TPU v7x, 32 devices: a whole 2x2x4 slice. The times are simulated.
32 devices in a mesh: dp: 16 (over z, y, x), tp: 2 (over core).
Axes of the slice: x: 2, y: 2, z: 4, core: 2. Of those that a mesh axis runs over, the one named last changes fastest.
Arguments:
- inputs: bfloat16 [50688, 384], P(('dp', 'tp')), may hold values from -6 to 6
- keep_mask: int32 [50688], P('dp'), may hold values from 0 to 1, as said below
- cotangent: bfloat16 [50688, 384], P(('dp', 'tp')), may hold values from -6 to 6
- qkv_master: float32 [3, 384, 384], P(None, 'dp', 'tp'), may hold values from -0.3125 to 0.3125
- qkv_first: float32 [3, 384, 384], P(None, 'dp', 'tp'), may hold values from -160 to 160
- qkv_second: float32 [3, 384, 384], P(None, 'dp', 'tp'), may hold values from 25.344 to 405.504
- proj_master: float32 [384, 384], P('tp', 'dp'), may hold values from -3.5 to 3.5
- proj_first: float32 [384, 384], P('tp', 'dp'), may hold values from -24 to 24
- proj_second: float32 [384, 384], P('tp', 'dp'), may hold values from 0.57024 to 9.12384
- fc1_master: float32 [384, 1536], P('dp', 'tp'), may hold values from -0.3125 to 0.3125
- fc1_first: float32 [384, 1536], P('dp', 'tp'), may hold values from -64 to 64
- fc1_second: float32 [384, 1536], P('dp', 'tp'), may hold values from 4.05504 to 64.88064
- fc2_master: float32 [1536, 384], P('tp', 'dp'), may hold values from -0.15625 to 0.15625
- fc2_first: float32 [1536, 384], P('tp', 'dp'), may hold values from -112 to 112
- fc2_second: float32 [1536, 384], P('tp', 'dp'), may hold values from 12.41856 to 198.69696
- norm_master: float32 [6, 384], replicated, may hold values from -4 to 4, as said below
- norm_first: float32 [6, 384], replicated, may hold values from -224 to 224
- norm_second: float32 [6, 384], replicated, may hold values from 57.024 to 912.384
- bias_master: float32 [2, 1152], P('tp'), may hold values from -6 to 6
- bias_first: float32 [2, 1152], P('tp'), may hold values from -160 to 160
- bias_second: float32 [2, 1152], P('tp'), may hold values from 25.344 to 405.504
Outputs:
- output: bfloat16 [50688, 384], P(('dp', 'tp'))
- grad_inputs: float32 [50688, 384], P(('dp', 'tp'))
- qkv_first_new: float32 [3, 384, 384], P(None, 'dp', 'tp')
- qkv_second_new: float32 [3, 384, 384], P(None, 'dp', 'tp')
- qkv_master_new: float32 [3, 384, 384], P(None, 'dp', 'tp')
- qkv_copy: bfloat16 [3, 384, 384], P(None, 'dp', 'tp')
- proj_first_new: float32 [384, 384], P('tp', 'dp')
- proj_second_new: float32 [384, 384], P('tp', 'dp')
- proj_master_new: float32 [384, 384], P('tp', 'dp')
- proj_copy: bfloat16 [384, 384], P('tp', 'dp')
- fc1_first_new: float32 [384, 1536], P('dp', 'tp')
- fc1_second_new: float32 [384, 1536], P('dp', 'tp')
- fc1_master_new: float32 [384, 1536], P('dp', 'tp')
- fc1_copy: bfloat16 [384, 1536], P('dp', 'tp')
- fc2_first_new: float32 [1536, 384], P('tp', 'dp')
- fc2_second_new: float32 [1536, 384], P('tp', 'dp')
- fc2_master_new: float32 [1536, 384], P('tp', 'dp')
- fc2_copy: bfloat16 [1536, 384], P('tp', 'dp')
- norm_first_new: float32 [6, 384], replicated
- norm_second_new: float32 [6, 384], replicated
- norm_master_new: float32 [6, 384], replicated
- bias_first_new: float32 [2, 1152], P('tp')
- bias_second_new: float32 [2, 1152], P('tp')
- bias_master_new: float32 [2, 1152], P('tp')
Inputs may be any that keep to these rules, and one draw needn't show every extreme that they name: `keep_mask`: 1 keeps a token, 0 drops it; the first two tokens of each image of 198 (class and distillation) are always kept. `norm_master`: rows 0 and 2 lie between 0.6 and 1.4.
All inputs are finite; a program needn't handle non-finite values.
Results may differ from a plain program's by a relative error of at most 0.012.
The roundings to bfloat16 on the way count: a program that leaves them out, or rounds other values in their place, can miss the bound.
Values may be sent and summed in bfloat16 or wider, within the bound.
A program may use at most 128 MiB of HBM per device.

v0:
```python
import functools

import jax
import jax.numpy as jnp
from jax import lax
from jax.experimental import pallas as pl
from jax.experimental.pallas import tpu as pltpu
from jax.sharding import PartitionSpec as P

HEAD_DIM = 64
PATCHES = 196
STEP = 5

norm_eps = 1e-06
beta_one = 0.9
beta_two = 0.999
adam_eps = 1e-08
matrix_decay = 0.05

F32 = jnp.float32
BF16 = jnp.bfloat16
MESH = pl.DeviceIdType.MESH
SEQ = PATCHES + 2
PAD = 208
WIDE = 256
NEG = -1000000000.0
SCALE = HEAD_DIM**-0.5
G_QKV, G_MID, G_FF, G_BACK, G_LAST, G_OUT = 8, 4, 8, 4, 4, 4
U_ATT, U_ATB = 8, 4


def dot_nn(a, b):
    return lax.dot_general(a, b, (((1,), (0,)), ((), ())), preferred_element_type=F32)


def dot_nt(a, b):
    return lax.dot_general(a, b, (((1,), (1,)), ((), ())), preferred_element_type=F32)


def dot_tn(a, b):
    return lax.dot_general(a, b, (((0,), (0,)), ((), ())), preferred_element_type=F32)


def norm_parts(v):
    mean = jnp.mean(v, axis=-1, keepdims=True)
    centred = v - mean
    var = jnp.mean(centred * centred, axis=-1, keepdims=True)
    rstd = lax.rsqrt(var + norm_eps)
    return centred * rstd, rstd


def norm_back(grad, xhat, rstd, gain):
    u = grad * gain
    return (
        u
        - jnp.mean(u, axis=-1, keepdims=True)
        - xhat * jnp.mean(u * xhat, axis=-1, keepdims=True)
    ) * rstd


def gelu_parts(u):
    cdf = 0.5 + 0.5 * lax.erf(0.7071067811865476 * u)
    return u * cdf, cdf + u * (0.3989422804014327 * jnp.exp(-0.5 * u * u))


def adam(master, first, second, grad, rate, decay):
    first = beta_one * first + (1.0 - beta_one) * grad
    second = beta_two * second + (1.0 - beta_two) * grad * grad
    first_hat = first / (1.0 - beta_one**STEP)
    second_hat = second / (1.0 - beta_two**STEP)
    master = master - rate * (first_hat / (jnp.sqrt(second_hat) + adam_eps) + decay * master)
    return first, second, master


def piece_parts(kind, tt, width):
    if kind == "a":
        return [(b // 2, 64 * (b % 2), 64, 128 * b + 64 * tt) for b in range(4)]
    return [(0, 0, width, width * tt), (1, 0, width, 2 * width + width * tt)]


def kernel(
    nl,
    np_,
    x_h,
    keep_h,
    cot_h,
    qm_h,
    pm_h,
    am_h,
    cm_h,
    nm_h,
    bm_h,
    out_h,
    gin_h,
    fin_a,
    fin_m,
    vec_o,
    kept_o,
    keep_v,
    qm,
    pm,
    am,
    cm,
    nm,
    bm,
    wba,
    wbm,
    w_qkv,
    w_proj,
    w_up,
    w_down,
    grd,
    sib_a,
    sib_m,
    rpl_a,
    rpl_m,
    lsn_a,
    lsn_m,
    rln_a,
    rln_m,
    pk_a,
    pk_m,
    bias2,
    cntl,
    cntp,
    biases,
    hid,
    vec,
    vsib,
    vpl,
    vln,
    stage,
    mid,
    gmid,
    probs,
    even,
    odd,
    mcol,
    mkt,
    xpad,
    back,
    n1,
    qkv,
    att,
    n2,
    gbr,
    gatt,
    act,
    gp,
    dqkv,
    dma_sem,
    in_sem,
    ag_s,
    ag_lr,
    ag_pr,
    ag_cr,
    rs_ss,
    rs_sr,
    rs_ps,
    rs_pr,
    rs_ls,
    rs_lr,
    cn_s,
    cn_r,
    cm_s,
    cm_r,
    vs_s,
    vs_r,
):
    rows, dim = x_h.shape
    images = rows // SEQ
    r = qm.shape[1]
    hw = qm.shape[2]
    width = wbm.shape[3]
    chunks = wbm.shape[0]
    chunk = 2 * width
    heads = dim // HEAD_DIM
    pairs = heads // 2
    t = lax.axis_index("tp")
    d = lax.axis_index("dp")
    l = d // np_
    p = d - l * np_
    o = 1 - t

    line_peer = [lax.rem(l + k, nl) for k in range(nl)]
    line_from = [lax.rem(l + nl - k, nl) for k in range(nl)]
    plane_peer = [lax.rem(p + k, np_) for k in range(np_)]
    plane_from = [lax.rem(p + np_ - k, np_) for k in range(np_)]
    line_dev = [{"dp": ll * np_ + p} for ll in line_peer]
    plane_dev = [{"dp": l * np_ + pp} for pp in plane_peer]
    other_core = {"tp": o}
    block = nl * np_

    def slot_at(tt, pp, ll):
        return tt * block + pp * nl + ll

    own_slot = slot_at(t, p, l)

    x_in = pltpu.make_async_copy(x_h, dqkv.at[0:rows, 0:dim], dma_sem.at[0])
    c_in = pltpu.make_async_copy(cot_h, dqkv.at[0:rows, dim : 2 * dim], dma_sem.at[1])
    small_in = [
        pltpu.make_async_copy(src, dst, in_sem.at[k])
        for k, (src, dst) in enumerate(
            ((qm_h, qm), (pm_h, pm), (am_h, am), (cm_h, cm), (bm_h, bm), (keep_h, keep_v), (nm_h, nm))
        )
    ]
    for cp in small_in:
        cp.start()
    x_in.start()
    c_in.start()

    barrier = pltpu.get_barrier_semaphore()
    for k in range(1, nl):
        pl.semaphore_signal(barrier, inc=1, device_id=line_dev[k], device_id_type=MESH)
    for k in range(1, np_):
        pl.semaphore_signal(barrier, inc=1, device_id=plane_dev[k], device_id_type=MESH)
    pl.semaphore_signal(barrier, inc=1, device_id=other_core, device_id_type=MESH)

    def kind_of(pc):
        return ("a", pc) if pc < pairs else ("m", pc - pairs)

    def of(piece, a_ref, m_ref):
        kind, at = piece
        return a_ref.at[at] if kind == "a" else m_ref.at[at]

    def w_buf(piece):
        return of(piece, wba, wbm)

    def sem_of(piece):
        kind, at = piece
        return at if kind == "a" else pairs + at

    def stacked(kind, blocks):
        pk = pk_a if kind == "a" else pk_m
        have, need = r * len(blocks), pk.shape[0]
        if r % 8 == 0:
            pad = [jnp.zeros((need - have, pk.shape[1]), F32)] if need > have else []
            return jnp.concatenate(list(blocks) + pad, axis=0)
        if need > have:
            pk[...] = jnp.zeros_like(pk)
        for b, block in enumerate(blocks):
            pk[b * r : (b + 1) * r, :] = block
        return pk[...]

    for cp in small_in:
        cp.wait()
    for c in range(pairs):
        cols = slice(64 * c, 64 * c + 64)
        wba[c, own_slot] = stacked(
            "a",
            [
                jnp.concatenate([qm[0, :, cols], qm[1, :, cols]], axis=1),
                jnp.concatenate([qm[2, :, cols], pm[:, cols]], axis=1),
            ],
        ).astype(BF16)
    for j in range(chunks):
        cols = slice(j * width, (j + 1) * width)
        wbm[j, own_slot] = stacked("m", [am[:, cols], cm[:, cols]]).astype(BF16)
    bias2[t] = jnp.broadcast_to(bm[...], bias2.shape[1:])
    full = keep_v.shape[0] // 128
    tail = keep_v.shape[0] - full * 128
    mkt[...] = jnp.zeros_like(mkt)
    mkt[0:full, :] = keep_v[pl.ds(0, full * 128)].reshape(full, 128).astype(F32)
    if tail:
        mkt[full : full + 1, 0:tail] = keep_v[pl.ds(full * 128, tail)].reshape(1, tail).astype(F32)
    count = jnp.sum(jnp.sum(mkt[...], axis=1, keepdims=True), axis=0, keepdims=True)
    cntl[l] = jnp.broadcast_to(count, cntl.shape[1:])

    pl.semaphore_wait(barrier, nl - 1 + np_ - 1 + 1)

    def remote(src, dst, ssem, rsem, device):
        return pltpu.make_async_remote_copy(
            src_ref=src, dst_ref=dst, send_sem=ssem, recv_sem=rsem, device_id=device, device_id_type=MESH
        )

    def got(dst, rsem):
        return remote(dst, dst, dma_sem.at[2], rsem, other_core)

    sends = []

    def send(src, dst, ssem, rsem, device):
        cp = remote(src, dst, ssem, rsem, device)
        cp.start()
        sends.append(cp)

    def line_copy(piece, k):
        pc, here = sem_of(piece), w_buf(piece).at[own_slot]
        return remote(here, here, ag_s.at[pc], ag_lr.at[pc, k - 1], line_dev[k])

    def plane_copy(piece, kl, k):
        pc, here = sem_of(piece), w_buf(piece).at[slot_at(t, p, line_from[kl])]
        return remote(here, here, ag_s.at[pc], ag_pr.at[pc, k - 1], plane_dev[k])

    def core_copy(piece, k):
        pc, here = sem_of(piece), w_buf(piece).at[pl.ds(slot_at(t, plane_from[k], 0), nl)]
        return remote(here, here, ag_s.at[pc], ag_cr.at[pc], other_core)

    def own_to_plane(piece):
        for k in range(1, np_):
            plane_copy(piece, 0, k).start()

    def start_piece(pc):
        piece = kind_of(pc)
        for k in range(1, nl):
            line_copy(piece, k).start()
        if piece[0] == "a":
            own_to_plane(piece)

    def line_done(pc):
        piece = kind_of(pc)
        if piece[0] == "m":
            own_to_plane(piece)
        for k in range(1, nl):
            got(w_buf(piece).at[slot_at(t, p, line_from[k])], ag_lr.at[pc, k - 1]).wait_recv()
            for kp in range(1, np_):
                plane_copy(piece, k, kp).start()
        core_copy(piece, 0).start()

    def plane_done(pc):
        piece = kind_of(pc)
        for k in range(1, np_):
            got(w_buf(piece).at[pl.ds(slot_at(t, plane_from[k], 0), nl)], ag_pr.at[pc, k - 1]).wait_recv()
            core_copy(piece, k).start()

    def core_done(piece):
        got(w_buf(piece).at[pl.ds(o * block, block)], ag_cr.at[sem_of(piece)]).wait_recv()

    def gather_sent(piece):
        sent = w_buf(piece).at[pl.ds(0, 2 * block - 1)]
        remote(sent, sent, ag_s.at[sem_of(piece)], dma_sem.at[2], other_core).wait_send()

    def lanes(at, size):
        return pl.ds(pl.multiple_of(at * size, 128), size)

    def assemble(piece):
        kind, where = piece
        for tt in range(2):
            for ll in range(nl):
                for pp in range(np_):
                    slot = w_buf(piece)[slot_at(tt, pp, ll)].astype(F32)
                    row = (ll * np_ + pp) * r
                    for b, lane_at, cols, col in piece_parts(kind, tt, width):
                        grd[row : row + r, col : col + cols] = slot[b * r : (b + 1) * r, lane_at : lane_at + cols]
        if kind == "a":
            w_qkv[:, lanes(where, 384)] = grd[:, 0:384].astype(BF16)
            w_proj[:, lanes(where, 128)] = grd[:, 384:512].astype(BF16)
        else:
            w_up[:, lanes(where, chunk)] = grd[:, 0:chunk].astype(BF16)
            w_down[:, lanes(where, chunk)] = grd[:, chunk : 2 * chunk].astype(BF16)

    start_piece(0)
    send(bias2.at[t], bias2.at[t], cm_s.at[0], cm_r.at[0], other_core)
    for k in range(1, nl):
        send(cntl.at[l], cntl.at[l], cn_s.at[k], cn_r.at[k], line_dev[k])

    def cast_in(col):
        def step(c, carry):
            at_row = pl.ds(pl.multiple_of(c * 16, 16), 16)
            stage[at_row, :] = dqkv[at_row, col : col + dim].astype(F32)
            return carry

        lax.fori_loop(0, rows // 16, step, 0)

    stage[rows:, :] = jnp.zeros((stage.shape[0] - rows, dim), F32)
    mask_rows = mkt[...].astype(BF16)
    ones = jnp.ones((128, 128), BF16)
    row_id = lax.broadcasted_iota(jnp.int32, (PAD, 128), 0)
    lane_id = lax.broadcasted_iota(jnp.int32, (PAD, 128), 1)
    for i in range(images):
        token = row_id + (t * rows + i * SEQ)
        picked = dot_nn((lane_id == token // 128).astype(F32).astype(BF16), mask_rows)
        hit = (lane_id == token % 128) & (row_id < SEQ)
        mcol[i] = dot_nn(jnp.where(hit, picked, 0.0).astype(BF16), ones)
    inside = lax.broadcasted_iota(jnp.int32, (PAD, dim), 0) < SEQ
    x_in.wait()
    cast_in(0)
    gain1, shift1 = nm[0:1, :], nm[1:2, :]

    def norm_in(i):
        v = jnp.where(inside, stage[i * SEQ : i * SEQ + PAD, :], 0.0)
        xpad[i * PAD : (i + 1) * PAD, :] = v.astype(BF16)
        xhat, _ = norm_parts(v)
        n1[i * PAD : (i + 1) * PAD, :] = (xhat * gain1 + shift1).astype(BF16)

    def back_in(i):
        v = jnp.where(inside, stage[i * SEQ : i * SEQ + PAD, :], 0.0)
        m = mcol[i]
        back[i * PAD : (i + 1) * PAD, :] = (v * jnp.concatenate([m] * (dim // 128), axis=1)).astype(BF16)

    for i in range(images // 4):
        norm_in(i)
    line_done(0)
    start_piece(1)
    start_piece(2)
    start_piece(3)
    for k in range(1, nl):
        got(cntl.at[line_from[k]], cn_r.at[k]).wait_recv()
    cntp[p] = functools.reduce(lambda a, b: a + b, [cntl[ll] for ll in range(nl)])
    for k in range(1, np_):
        send(cntp.at[p], cntp.at[p], cm_s.at[k], cm_r.at[k], plane_dev[k])
    for i in range(images // 4, images):
        norm_in(i)
    line_done(1)
    plane_done(0)
    c_in.wait()
    cast_in(dim)
    for i in range(images):
        back_in(i)
    core_done(kind_of(0))
    got(bias2.at[o], cm_r.at[0]).wait_recv()
    assemble(kind_of(0))

    def image_rows(i, many=1):
        return pl.ds(pl.multiple_of(i * (many * PAD), 16), many * PAD)

    def over_images(step, many=1, unroll=1):
        lax.fori_loop(0, images // many, lambda i, carry: step(i) or carry, 0, unroll=unroll)

    both = [bias2[0, 0:1, :], bias2[1, 0:1, :]]
    for j in range(chunks):
        parts = [b[:, 2 * hw + j * width : 2 * hw + (j + 1) * width] for b in both]
        biases[1:2, j * chunk : (j + 1) * chunk] = jnp.concatenate(parts, axis=1)
    for c in range(pairs):
        parts = [b[:, 64 * c : 64 * c + 64] for b in both] + [jnp.zeros((1, 128), F32)]
        parts += [b[:, hw + 64 * c : hw + 64 * c + 64] for b in both]
        biases[0:1, 384 * c : 384 * c + 384] = jnp.concatenate(parts, axis=1)

    def qkv_rows(c):
        cols = lanes(c, 384)

        def step(i):
            here = image_rows(i, G_QKV)
            qkv[here, cols] = (dot_nn(n1[here, :], w_qkv[:, cols]) + biases[0:1, cols]).astype(BF16)

        over_images(step, G_QKV)

    lane = lax.broadcasted_iota(jnp.int32, (1, 128), 1)
    head_mask = [(lane < HEAD_DIM).astype(F32).astype(BF16), (lane >= HEAD_DIM).astype(F32).astype(BF16)]
    head_scale = [(SCALE * mask.astype(F32)).astype(BF16) for mask in head_mask]

    def both_heads(v, scales):
        gap = jnp.zeros((WIDE - PAD, 128), BF16)
        return jnp.concatenate([v * scales[0], gap, v * scales[1], gap], axis=0)

    def of_heads(v):
        return v[:, 0:PAD], v[:, WIDE : WIDE + PAD]

    def pair_rows(ref, here, c, b):
        return ref[here, lanes(3 * c + b, 128)]

    def attend(c):
        def step(i):
            here = image_rows(i)
            qp, kp, vp = (pair_rows(qkv, here, c, b) for b in range(3))
            open_key = jnp.concatenate([mcol[i]] * (2 * WIDE // 128), axis=1) > 0.0
            s = jnp.where(open_key, dot_nt(kp, both_heads(qp, head_scale)), NEG)
            e = jnp.exp(s - jnp.max(s, axis=0, keepdims=True))
            pr = (e * (1.0 / jnp.sum(e, axis=0, keepdims=True))).astype(BF16)
            probs[i * pairs + c] = pr
            first, second = of_heads(pr)
            total = dot_tn(first, vp * head_mask[0]) + dot_tn(second, vp * head_mask[1])
            att[here, lanes(c, 128)] = total.astype(BF16)

        over_images(step, unroll=U_ATT)

    def pair_forward(c, carry):
        qkv_rows(c)

        @pl.when(c == 0)
        def _():
            line_done(2)
            line_done(3)
            plane_done(1)
            start_piece(4)

        @pl.when(c == 1)
        def _():
            plane_done(2)
            start_piece(5)

        @pl.when(c == 2)
        def _():
            line_done(4)

        attend(c)

        @pl.when(c < pairs - 1)
        def _():
            core_done(("a", c + 1))
            assemble(("a", c + 1))

        return carry

    lax.fori_loop(0, pairs, pair_forward, 0)
    plane_done(3)
    line_done(5)
    for k in range(1, np_):
        got(cntp.at[plane_from[k]], cm_r.at[k]).wait_recv()
    kept = functools.reduce(lambda a, b: a + b, [cntp[pp] for pp in range(np_)])
    grad_scale = (rows * 2.0 * nl * np_) / kept[0:1, 0:1]

    vec[...] = jnp.zeros_like(vec)
    hid[...] = jnp.zeros_like(hid)
    bias4, gain2, shift2, bias5 = nm[4:5, :], nm[2:3, :], nm[3:4, :], nm[5:6, :]

    def mid_step(i):
        here = image_rows(i, G_MID)
        m = xpad[here, :].astype(F32) + (dot_nt(att[here, :], w_proj[...]) + bias4)
        mid[here, :] = m
        xhat, _ = norm_parts(m)
        n2[here, :] = (xhat * gain2 + shift2).astype(BF16)

    over_images(mid_step, G_MID)

    def pack(piece):
        gather_sent(piece)
        kind = piece[0]
        for tt in range(2):
            parts = piece_parts(kind, tt, width)
            for ll in range(nl):
                for pp in range(np_):
                    row = (ll * np_ + pp) * r
                    blocks = []
                    for b in range(2):
                        own = [grd[row : row + r, col : col + cols] for bb, _, cols, col in parts if bb == b]
                        blocks.append(jnp.concatenate(own, axis=1) if len(own) > 1 else own[0])
                    w_buf(piece)[slot_at(tt, pp, ll)] = stacked(kind, blocks).astype(BF16)

    def sib_copy(piece):
        pc, src = sem_of(piece), w_buf(piece).at[pl.ds(o * block, block)]
        return remote(src, of(piece, sib_a, sib_m), rs_ss.at[pc], rs_sr.at[pc], other_core)

    def sum_plane_copy(piece, k):
        pc, src, dst = sem_of(piece), of(piece, sib_a, sib_m), of(piece, rpl_a, rpl_m)
        return remote(
            src.at[pl.ds(plane_peer[k] * nl, nl)], dst.at[pl.ds(p * nl, nl)], rs_ps.at[pc], rs_pr.at[pc], plane_dev[k]
        )

    def sum_line_copy(piece, k):
        pc, src, dst = sem_of(piece), of(piece, lsn_a, lsn_m), of(piece, rln_a, rln_m)
        return remote(src.at[line_peer[k]], dst.at[l], rs_ls.at[pc], rs_lr.at[pc], line_dev[k])

    def send_plane(piece):
        sib, rpl = of(piece, sib_a, sib_m), of(piece, rpl_a, rpl_m)
        got(sib, rs_sr.at[sem_of(piece)]).wait_recv()
        for at in range(block):
            sib[at] = (sib[at].astype(F32) + w_buf(piece)[t * block + at].astype(F32)).astype(BF16)
        for k in range(1, np_):
            sum_plane_copy(piece, k).start()
        own = pl.ds(p * nl, nl)
        rpl[own] = sib[own]

    def send_line(piece):
        rpl, lsn, rln = of(piece, rpl_a, rpl_m), of(piece, lsn_a, lsn_m), of(piece, rln_a, rln_m)
        got(rpl.at[pl.ds(0, (np_ - 1) * nl)], rs_pr.at[sem_of(piece)]).wait_recv()
        for ll in range(nl):
            lsn[ll] = functools.reduce(
                lambda a, b: a + b, [rpl[pp * nl + ll].astype(F32) for pp in range(np_)]
            ).astype(BF16)
        for k in range(1, nl):
            sum_line_copy(piece, k).start()
        rln[l] = lsn[l]

    def sum_line(piece):
        rln, fin = of(piece, rln_a, rln_m), of(piece, fin_a, fin_m)
        got(rln.at[pl.ds(0, nl - 1)], rs_lr.at[sem_of(piece)]).wait_recv()
        fin[...] = functools.reduce(lambda a, b: a + b, [rln[ll].astype(F32) for ll in range(nl)])

    def sums_sent(piece):
        pc = sem_of(piece)
        sib_copy(piece).wait_send()
        for sent, sem in (
            (of(piece, sib_a, sib_m).at[pl.ds(0, (np_ - 1) * nl)], rs_ps),
            (of(piece, lsn_a, lsn_m).at[pl.ds(0, nl - 1)], rs_ls),
        ):
            remote(sent, sent, sem.at[pc], dma_sem.at[2], other_core).wait_send()

    def ff_chunk(j):
        def step(i):
            here = image_rows(i, G_FF)
            b = back[here, :]
            cols = lanes(j, chunk)
            pre = dot_nn(n2[here, :], w_up[:, cols]) + biases[1:2, cols]
            ga = dot_nn(b, w_down[:, cols])
            value, slope = gelu_parts(pre)
            act[here, cols] = value.astype(BF16)
            gpre = (ga * slope).astype(BF16)
            gp[here, cols] = gpre
            hid[0:1, cols] += jnp.sum(gpre.astype(F32), axis=0, keepdims=True)

        over_images(step, G_FF)

    def ff_grad(j):
        cols = lanes(j, chunk)
        grd[:, 0:chunk] = dot_tn(n2[...], gp[:, cols])
        grd[:, chunk : 2 * chunk] = dot_tn(back[...], act[:, cols])

    def chunk_step(j, carry):
        core_done(("m", j))
        assemble(("m", j))
        ff_chunk(j)

        @pl.when(j == 0)
        def _():
            plane_done(4)

        @pl.when(j == 1)
        def _():
            plane_done(5)

        @pl.when(j > 1)
        def _():
            send_line(("m", j - 2))

        @pl.when(j > 0)
        def _():
            send_plane(("m", j - 1))

        ff_grad(j)
        pack(("m", j))
        sib_copy(("m", j)).start()
        return carry

    lax.fori_loop(0, chunks, chunk_step, 0)
    for j in range(chunks):
        vec[8 + j : 9 + j, :] = hid[0:1, j * chunk : (j + 1) * chunk]

    def back_step(i):
        here = image_rows(i, G_BACK)
        m = mid[here, :]
        xhat, rstd = norm_parts(m)
        dn = dot_nt(gp[here, :], w_up[...])
        bfl = back[here, :].astype(F32)
        gm = bfl + norm_back(dn, xhat, rstd, gain2)
        gmid[here, :] = gm
        g16 = gm.astype(BF16)
        gbr[here, :] = g16
        gatt[here, :] = dot_nn(g16, w_proj[...]).astype(BF16)
        vec[2:3, 0:dim] += jnp.sum(dn * xhat, axis=0, keepdims=True)
        vec[3:4, 0:dim] += jnp.sum(dn, axis=0, keepdims=True)
        vec[4:5, 0:dim] += jnp.sum(g16.astype(F32), axis=0, keepdims=True)
        vec[5:6, 0:dim] += jnp.sum(bfl, axis=0, keepdims=True)

    over_images(back_step, G_BACK)

    def attend_back(c):
        cols = lanes(c, 128)

        def start(i, into):
            here = image_rows(i)
            into[...] = dot_nt(pair_rows(qkv, here, c, 2), both_heads(gatt[here, cols], head_mask))

        def finish(i, dp_ref):
            here = image_rows(i)
            qp, kp = pair_rows(qkv, here, c, 0), pair_rows(qkv, here, c, 1)
            pr = probs[i * pairs + c]
            prf = pr.astype(F32)
            dp = dp_ref[...]
            inner = jnp.sum(prf * dp, axis=0, keepdims=True)
            ds = (prf * (dp - inner)).astype(BF16)
            dv = dot_nn(pr, both_heads(gatt[here, cols], head_mask)).astype(BF16)
            dk = dot_nn(ds, both_heads(qp, head_scale)).astype(BF16)
            first, second = of_heads(ds)
            dq = (dot_tn(first, kp * head_scale[0]) + dot_tn(second, kp * head_scale[1])).astype(BF16)
            for b, grad in enumerate((dq, dk, dv)):
                dqkv[here, lanes(3 * c + b, 128)] = grad
            vec[6:7, cols] += jnp.sum(dq.astype(F32), axis=0, keepdims=True)
            vec[7:8, cols] += jnp.sum(dv.astype(F32), axis=0, keepdims=True)

        start(0, even)

        def step(k):
            start(2 * k + 1, odd)
            finish(2 * k, even)
            start(jnp.minimum(2 * k + 2, images - 1), even)
            finish(2 * k + 1, odd)

        over_images(step, 2, unroll=U_ATB)

    def qkv_grad(c):
        grd[:, 0:384] = dot_tn(n1[...], dqkv[:, lanes(c, 384)])
        grd[:, 384:512] = dot_tn(gbr[...], att[:, lanes(c, 128)])
        pack(("a", c))
        sib_copy(("a", c)).start()

    send_plane(("m", 2))

    def pair_back(c, carry):
        attend_back(c)

        @pl.when(c == 0)
        def _():
            send_line(("m", 1))

        @pl.when(c > 0)
        def _():
            send_plane(("a", c - 1))

        @pl.when(c == 1)
        def _():
            send_line(("m", 2))

        qkv_grad(c)
        return carry

    lax.fori_loop(0, pairs, pair_back, 0)
    send_line(("a", 0))

    def last_step(i):
        here = image_rows(i, G_LAST)
        dn = dot_nt(dqkv[here, :], w_qkv[...])
        xhat, rstd = norm_parts(xpad[here, :].astype(F32))
        gmid[here, :] = (gmid[here, :] + norm_back(dn, xhat, rstd, gain1)) * grad_scale
        vec[0:1, 0:dim] += jnp.sum(dn * xhat, axis=0, keepdims=True)
        vec[1:2, 0:dim] += jnp.sum(dn, axis=0, keepdims=True)

    first_part = images // G_LAST // 2
    lax.fori_loop(0, first_part, lambda i, carry: last_step(i) or carry, 0)
    send_plane(("a", 2))
    lax.fori_loop(first_part, images // G_LAST, lambda i, carry: last_step(i) or carry, 0)
    send(vec, vsib, vs_s.at[0], vs_r.at[0], other_core)

    for i in range(images):
        stage[i * SEQ : (i + 1) * SEQ, :] = gmid[i * PAD : i * PAD + SEQ, :]
    gin_cp = pltpu.make_async_copy(stage.at[0:rows, :], gin_h, dma_sem.at[1])
    gin_cp.start()
    got(vsib, vs_r.at[0]).wait_recv()
    vpl[p] = vec[...] + vsib[...]
    for k in range(1, np_):
        send(vpl.at[p], vpl.at[p], vs_s.at[k], vs_r.at[k], plane_dev[k])
    send_line(("a", 1))

    def out_step(i):
        here = image_rows(i, G_OUT)
        mid[here, :] = mid[here, :] + (dot_nt(act[here, :], w_down[...]) + bias5)

    half_out = images // G_OUT // 2
    lax.fori_loop(0, half_out, lambda i, carry: out_step(i) or carry, 0)
    send_line(("a", 2))
    for k in range(1, np_):
        got(vpl.at[plane_from[k]], vs_r.at[k]).wait_recv()
    vln[l] = functools.reduce(lambda a, b: a + b, [vpl[pp] for pp in range(np_)])
    for k in range(1, nl):
        send(vln.at[l], vln.at[l], vs_s.at[np_ + k], vs_r.at[np_ + k], line_dev[k])
    lax.fori_loop(half_out, images // G_OUT, lambda i, carry: out_step(i) or carry, 0)
    for i in range(images):
        gmid[i * SEQ : (i + 1) * SEQ, :] = mid[i * PAD : i * PAD + SEQ, :]

    def cast_out(c, carry):
        at_row = pl.ds(pl.multiple_of(c * 16, 16), 16)
        n2[at_row, :] = gmid[at_row, :].astype(BF16)
        return carry

    lax.fori_loop(0, rows // 16, cast_out, 0)
    out_cp = pltpu.make_async_copy(n2.at[0:rows, :], out_h, dma_sem.at[0])
    out_cp.start()
    kept_o[...] = kept
    for pc in list(range(pairs, pairs + chunks)) + list(range(pairs)):
        sum_line(kind_of(pc))
    for k in range(1, nl):
        got(vln.at[line_from[k]], vs_r.at[np_ + k]).wait_recv()
    vec_o[...] = functools.reduce(lambda a, b: a + b, [vln[ll] for ll in range(nl)])
    out_cp.wait()
    gin_cp.wait()
    for pc in range(pairs + chunks):
        sums_sent(kind_of(pc))
    for cp in sends:
        cp.wait_send()


def update_kernel(scale_rows, *refs):
    ins, outs, kept_vm = refs[:24], refs[24:48], refs[48:]
    out_in, gin_in = ins[4:6]
    out_h, gin_h = outs[:2]
    small_in = ins[:4] + ins[6:]
    in_v, out_v = kept_vm[:22], list(kept_vm[22:40])
    big_out, big_gin, sems_in, sems_out, sems_a, sems_b = kept_vm[40:]
    copies = (3, 7, 11, 15)
    for k in copies:
        out_v.insert(k, outs[2 + k])
    parts = 3
    size = out_in.shape[0] // parts
    loads, stores = [], []
    for k in range(parts):
        here = pl.ds(k * size, size)
        for j, (src, via, dst) in enumerate(((out_in, big_out, out_h), (gin_in, big_gin, gin_h))):
            loads.append(pltpu.make_async_copy(src.at[here, :], via.at[here, :], sems_in.at[j, k]))
            stores.append(pltpu.make_async_copy(via.at[here, :], dst.at[here, :], sems_out.at[j, k]))
    small = [pltpu.make_async_copy(src, dst, sems_a.at[k]) for k, (src, dst) in enumerate(zip(small_in, in_v))]
    for cp in small + loads:
        cp.start()
    for cp in small:
        cp.wait()
    fin_a, fin_m, vec, kept = in_v[:4]
    states = [in_v[4 + 3 * k : 7 + 3 * k] for k in range(6)]
    results = [pltpu.make_async_copy(src, dst, sems_b.at[k]) for k, (src, dst) in enumerate(zip(out_v, outs[2:])) if k not in copies]
    q_o, p_o, a_o, c_o = (out_v[4 * k : 4 * k + 4] for k in range(4))
    n_o, b_o = out_v[16:19], out_v[19:22]
    qkv, proj, fc1, fc2, norm, bias = states
    r, hw = proj[0].shape
    chunks, _, width = fin_m.shape
    own = lax.axis_index("tp") == 0
    grad_scale = scale_rows / kept[0:1, 0:1]

    def update(grad, state, outs, rate, decay, c=None):
        pick = (lambda ref: ref[...]) if c is None else (lambda ref: ref[c])
        master, first, second = (pick(ref) for ref in state)
        first, second, master = adam(master, first, second, grad * grad_scale, rate, decay)
        for ref, value in zip(outs, (first, second, master, master)):
            if c is None:
                ref[...] = value.astype(ref.dtype)
            else:
                ref[c] = value.astype(ref.dtype)

    pairs = fin_a.shape[0]

    def over_pairs(block, lane_at):
        return jnp.concatenate(
            [fin_a[c, block * r : (block + 1) * r, lane_at : lane_at + 64] for c in range(pairs)], axis=1
        )

    update(over_pairs(0, 0), qkv, q_o, 0.08, matrix_decay, 0)
    update(over_pairs(0, 64), qkv, q_o, 0.08, matrix_decay, 1)
    update(over_pairs(1, 0), qkv, q_o, 0.08, matrix_decay, 2)
    update(over_pairs(1, 64), proj, p_o, 0.8, matrix_decay)
    update(jnp.concatenate([fin_m[j, 0:r, :] for j in range(chunks)], axis=1), fc1, a_o, 0.08, matrix_decay)
    update(jnp.concatenate([fin_m[j, r : 2 * r, :] for j in range(chunks)], axis=1), fc2, c_o, 0.04, matrix_decay)
    update(vec[0:6, 0 : norm[0].shape[1]], norm, n_o, 0.5, 0.0)

    def pick(row, col, cols):
        return jnp.where(
            own, vec[row : row + 1, col : col + cols], vec[row : row + 1, col + cols : col + 2 * cols]
        )

    bias_parts = [pick(row, 128 * c, 64) for row in (6, 7) for c in range(pairs)]
    bias_parts += [pick(8 + j, 0, width) for j in range(chunks)]
    update(jnp.concatenate(bias_parts, axis=1), bias, b_o, 0.5, 0.0)
    for cp in results:
        cp.start()
    for load, store in zip(loads, stores):
        load.wait()
        store.start()
    for cp in results + stores:
        cp.wait()


def body(
    inputs, keep_mask, cotangent,
    qkv_master, qkv_first, qkv_second,
    proj_master, proj_first, proj_second,
    fc1_master, fc1_first, fc1_second,
    fc2_master, fc2_first, fc2_second,
    norm_master, norm_first, norm_second,
    bias_master, bias_first, bias_second,
):
    n = lax.axis_size("dp")
    nl = 4 if n % 4 == 0 else n
    np_ = n // nl
    rows, dim = inputs.shape
    images = rows // SEQ
    padded = images * PAD
    r = qkv_master.shape[1]
    hw = qkv_master.shape[2]
    fw = fc1_master.shape[1]
    width = 256
    chunks = fw // width
    chunk = 2 * width
    slot_a = -(-2 * r // 16) * 16
    pairs = dim // HEAD_DIM // 2
    slot_m = -(-2 * r // 16) * 16
    vm = pl.BlockSpec(memory_space=pltpu.VMEM)
    hbm = pl.BlockSpec(memory_space=pl.ANY)

    def like(a, dtype=None):
        return jax.ShapeDtypeStruct(a.shape, dtype or a.dtype)

    proj_master, proj_first, proj_second = proj_master.T, proj_first.T, proj_second.T
    fc2_master, fc2_first, fc2_second = fc2_master.T, fc2_first.T, fc2_second.T
    large = [like(inputs), like(inputs, F32)]
    sums = [
        jax.ShapeDtypeStruct((pairs, slot_a, 128), F32),
        jax.ShapeDtypeStruct((chunks, slot_m, width), F32),
        jax.ShapeDtypeStruct((16, chunk), F32),
        jax.ShapeDtypeStruct((8, 128), F32),
    ]
    dma = pltpu.SemaphoreType.DMA
    pieces = pairs + chunks
    small = (keep_mask, qkv_master, proj_master, fc1_master, fc2_master, norm_master, bias_master)
    scratch = [pltpu.VMEM(a.shape, a.dtype) for a in small] + [
        pltpu.VMEM((pairs, 2 * np_ * nl, slot_a, 128), BF16),
        pltpu.VMEM((chunks, 2 * np_ * nl, slot_m, width), BF16),
        pltpu.VMEM((dim, 3 * dim), BF16),
        pltpu.VMEM((dim, dim), BF16),
        pltpu.VMEM((dim, chunks * chunk), BF16),
        pltpu.VMEM((dim, chunks * chunk), BF16),
        pltpu.VMEM((dim, 2 * chunk), F32),
        pltpu.VMEM((pairs, np_ * nl, slot_a, 128), BF16),
        pltpu.VMEM((chunks, np_ * nl, slot_m, width), BF16),
        pltpu.VMEM((pairs, np_ * nl, slot_a, 128), BF16),
        pltpu.VMEM((chunks, np_ * nl, slot_m, width), BF16),
        pltpu.VMEM((pairs, nl, slot_a, 128), BF16),
        pltpu.VMEM((chunks, nl, slot_m, width), BF16),
        pltpu.VMEM((pairs, nl, slot_a, 128), BF16),
        pltpu.VMEM((chunks, nl, slot_m, width), BF16),
        pltpu.VMEM((slot_a, 128), F32),
        pltpu.VMEM((slot_m, width), F32),
        pltpu.VMEM((2, 8, bias_master.shape[1]), F32),
        pltpu.VMEM((nl, 8, 128), F32),
        pltpu.VMEM((np_, 8, 128), F32),
        pltpu.VMEM((8, chunks * chunk), F32),
        pltpu.VMEM((8, chunks * chunk), F32),
        pltpu.VMEM((16, chunk), F32),
        pltpu.VMEM((16, chunk), F32),
        pltpu.VMEM((np_, 16, chunk), F32),
        pltpu.VMEM((nl, 16, chunk), F32),
        pltpu.VMEM((-(-(rows - SEQ + PAD) // 16) * 16, dim), F32),
        pltpu.VMEM((padded, dim), F32),
        pltpu.VMEM((padded, dim), F32),
        pltpu.VMEM((images * pairs, PAD, 2 * WIDE), BF16),
        pltpu.VMEM((PAD, 2 * WIDE), F32),
        pltpu.VMEM((PAD, 2 * WIDE), F32),
        pltpu.VMEM((images, PAD, 128), F32),
        pltpu.VMEM((128, 128), F32),
        pltpu.VMEM((padded, dim), BF16),
        pltpu.VMEM((padded, dim), BF16),
        pltpu.VMEM((padded, dim), BF16),
        pltpu.VMEM((padded, 3 * dim), BF16),
        pltpu.VMEM((padded, dim), BF16),
        pltpu.VMEM((padded, dim), BF16),
        pltpu.VMEM((padded, dim), BF16),
        pltpu.VMEM((padded, dim), BF16),
        pltpu.VMEM((padded, chunks * chunk), BF16),
        pltpu.VMEM((padded, chunks * chunk), BF16),
        pltpu.VMEM((padded, 3 * dim), BF16),
        dma((3,)),
        dma((7,)),
        dma((pieces,)),
        dma((pieces, nl - 1)),
        dma((pieces, np_ - 1)),
        dma((pieces,)),
        dma((pieces,)),
        dma((pieces,)),
        dma((pieces,)),
        dma((pieces,)),
        dma((pieces,)),
        dma((pieces,)),
        dma((nl,)),
        dma((nl,)),
        dma((np_,)),
        dma((np_,)),
        dma((np_ + nl,)),
        dma((np_ + nl,)),
    ]
    out, gin, fin_a, fin_m, vec, kept = pl.pallas_call(
        functools.partial(kernel, nl, np_),
        out_shape=large + sums,
        in_specs=[hbm] * 9,
        out_specs=[hbm, hbm] + [vm] * 4,
        scratch_shapes=scratch,
        compiler_params=pltpu.CompilerParams(
            collective_id=0, has_side_effects=True, vmem_limit_bytes=64 * 1024 * 1024
        ),
    )(inputs, keep_mask, cotangent, qkv_master, proj_master, fc1_master, fc2_master, norm_master, bias_master)
    states = [
        qkv_master, qkv_first, qkv_second,
        proj_master, proj_first, proj_second,
        fc1_master, fc1_first, fc1_second,
        fc2_master, fc2_first, fc2_second,
        norm_master, norm_first, norm_second,
        bias_master, bias_first, bias_second,
    ]
    outs = list(large)
    for a in (qkv_master, proj_master, fc1_master, fc2_master):
        outs += [like(a), like(a), like(a), like(a, BF16)]
    for a in (norm_master, bias_master):
        outs += [like(a)] * 3
    res = list(
        pl.pallas_call(
            functools.partial(update_kernel, rows * 2.0 * n),
            out_shape=outs,
            in_specs=[hbm] * 24,
            out_specs=[vm if a.dtype == BF16 and k > 0 else hbm for k, a in enumerate(outs)],
            scratch_shapes=[pltpu.VMEM(a.shape, a.dtype) for a in sums + states + [a for a in outs[2:] if a.dtype == F32]]
            + [pltpu.VMEM((rows, dim), BF16), pltpu.VMEM((rows, dim), F32)]
            + [dma((2, 3)), dma((2, 3)), dma((22,)), dma((22,))],
            compiler_params=pltpu.CompilerParams(vmem_limit_bytes=64 * 1024 * 1024),
        )(fin_a, fin_m, vec, kept, out, gin, *states)
    )
    for k in (6, 7, 8, 9, 14, 15, 16, 17):
        res[k] = res[k].T
    return tuple(res)


def solution(mesh):
    mats = [P(None, "dp", "tp"), P("tp", "dp"), P("dp", "tp"), P("tp", "dp")]
    in_specs = [P(("dp", "tp"), None), P("dp"), P(("dp", "tp"), None)]
    out_specs = [P(("dp", "tp"), None), P(("dp", "tp"), None)]
    for m in mats:
        in_specs += [m] * 3
        out_specs += [m] * 4
    in_specs += [P()] * 3 + [P("tp", None)] * 3
    out_specs += [P()] * 3 + [P("tp", None)] * 3
    return jax.shard_map(
        body, mesh=mesh, in_specs=tuple(in_specs), out_specs=tuple(out_specs), check_vma=False
    )
```

profile of v0, /device:TPU:0, one launch (start us, length us, event | category | flops | bytes accessed | tf_op | source)
XLA Modules:
  0.0 80.9 jit_solution(4038048451334618040)
XLA Ops:
  0.7 74.6 %shard_map.388 = (bf16[1584,384]{1,0:T(8,128)(2,1)}, f32[1584,384]{1,0:T(8,128)}, f32[3,48,128]{2,1,0:T(8,128)}, f32[3,48,256]{2,1,0:T(8,128)}, f32[16,512]{1,0:T(8,128)}, /*index=5*/f32[8,128]{1,0:T(8,128)}) custom-call(bf16[1584,384]{1,0:T(8,128)(2,1)} %x_h.1, s32[3168]{0:T(1024)} %keep_h.1, bf16[1584,384]{1,0:T(8,128)(2,1)} %cot_h.1, ...), custom_call_target="tpu_custom_call" | custom-call | tf_op jit(solution)/shard_map/pallas_call | solution.py:954
  75.3 5.4 %shard_map.389 = (bf16[1584,384]{1,0:T(8,128)(2,1)}, f32[1584,384]{1,0:T(8,128)}, f32[3,24,192]{2,1,0:T(8,128)}, f32[3,24,192]{2,1,0:T(8,128)}, f32[3,24,192]{2,...) custom-call(f32[3,48,128]{2,1,0:T(8,128)} %get-tuple-element.54.refs, ...), custom_call_target="tpu_custom_call" | custom-call | tf_op jit(solution)/shard_map/pallas_call | solution.py:978
where the time goes:
time: 81 us; the launch traced here: 80.9 us
  Pallas kernels  80 us (99%)
  between operations  0.83 us (1%)
    pallas_call x1, Pallas kernels, body(): pl.pallas_call(functools.partial(kernel, nl, np_), out_shape=large + sums...  74.6 us
    pallas_call x1, Pallas kernels, body(): pl.pallas_call(functools.partial(update_kernel, rows * 2.0 * n), out_shap...  5.42 us

commit v1 on v0

--- a/solution.py
+++ b/solution.py
@@ -110,6 +110,7 @@
     w_up,
     w_down,
     grd,
+    gproj,
     sib_a,
     sib_m,
     rpl_a,
@@ -244,18 +245,18 @@
 
     for cp in small_in:
         cp.wait()
-    for c in range(pairs):
-        cols = slice(64 * c, 64 * c + 64)
-        wba[c, own_slot] = stacked(
-            "a",
-            [
-                jnp.concatenate([qm[0, :, cols], qm[1, :, cols]], axis=1),
-                jnp.concatenate([qm[2, :, cols], pm[:, cols]], axis=1),
-            ],
-        ).astype(BF16)
-    for j in range(chunks):
-        cols = slice(j * width, (j + 1) * width)
-        wbm[j, own_slot] = stacked("m", [am[:, cols], cm[:, cols]]).astype(BF16)
+    def pack_own(pc):
+        kind, at = kind_of(pc)
+        if kind == "a":
+            cols = slice(64 * at, 64 * at + 64)
+            top = jnp.concatenate([qm[0, :, cols], qm[1, :, cols]], axis=1)
+            blocks = [top, jnp.concatenate([qm[2, :, cols], pm[:, cols]], axis=1)]
+        else:
+            cols = slice(at * width, (at + 1) * width)
+            blocks = [am[:, cols], cm[:, cols]]
+        w_buf((kind, at))[own_slot] = stacked(kind, blocks).astype(BF16)
+
+    pack_own(0)
     bias2[t] = jnp.broadcast_to(bm[...], bias2.shape[1:])
     full = keep_v.shape[0] // 128
     tail = keep_v.shape[0] - full * 128
@@ -353,6 +354,12 @@
     for k in range(1, nl):
         send(cntl.at[l], cntl.at[l], cn_s.at[k], cn_r.at[k], line_dev[k])
 
+    for pc in range(1, pairs):
+        pack_own(pc)
+        start_piece(pc)
+    for pc in range(pairs, pairs + chunks):
+        pack_own(pc)
+
     def cast_in(col):
         def step(c, carry):
             at_row = pl.ds(pl.multiple_of(c * 16, 16), 16)
@@ -390,17 +397,18 @@
     for i in range(images // 4):
         norm_in(i)
     line_done(0)
-    start_piece(1)
-    start_piece(2)
     start_piece(3)
+    for i in range(images // 4, images // 2):
+        norm_in(i)
+    line_done(1)
     for k in range(1, nl):
         got(cntl.at[line_from[k]], cn_r.at[k]).wait_recv()
     cntp[p] = functools.reduce(lambda a, b: a + b, [cntl[ll] for ll in range(nl)])
     for k in range(1, np_):
         send(cntp.at[p], cntp.at[p], cm_s.at[k], cm_r.at[k], plane_dev[k])
-    for i in range(images // 4, images):
+    line_done(2)
+    for i in range(images // 2, images):
         norm_in(i)
-    line_done(1)
     plane_done(0)
     c_in.wait()
     cast_in(dim)
@@ -468,8 +476,6 @@
 
         @pl.when(c == 0)
         def _():
-            line_done(2)
-            line_done(3)
             plane_done(1)
             start_piece(4)
 
@@ -491,6 +497,7 @@
 
         return carry
 
+    line_done(3)
     lax.fori_loop(0, pairs, pair_forward, 0)
     plane_done(3)
     line_done(5)
@@ -608,10 +615,6 @@
         def _():
             plane_done(5)
 
-        @pl.when(j > 1)
-        def _():
-            send_line(("m", j - 2))
-
         @pl.when(j > 0)
         def _():
             send_plane(("m", j - 1))
@@ -622,8 +625,35 @@
         return carry
 
     lax.fori_loop(0, chunks, chunk_step, 0)
-    for j in range(chunks):
-        vec[8 + j : 9 + j, :] = hid[0:1, j * chunk : (j + 1) * chunk]
+
+    def vec_copy(part, at):
+        ssem, rsem = vs_s.at[part, at], vs_r.at[part, at]
+        if at == 0:
+            return remote(vec.at[part], vsib.at[part], ssem, rsem, other_core)
+        if at < np_:
+            return remote(vpl.at[part, p], vpl.at[part, p], ssem, rsem, plane_dev[at])
+        return remote(vln.at[part, l], vln.at[part, l], ssem, rsem, line_dev[at - np_ + 1])
+
+    def vec_core(part):
+        vec_copy(part, 0).start()
+
+    def vec_plane(part):
+        got(vsib.at[part], vs_r.at[part, 0]).wait_recv()
+        vpl[part, p] = vec[part] + vsib[part]
+        for k in range(1, np_):
+            vec_copy(part, k).start()
+
+    def vec_line(part):
+        for k in range(1, np_):
+            got(vpl.at[part, plane_from[k]], vs_r.at[part, k]).wait_recv()
+        vln[part, l] = functools.reduce(lambda a, b: a + b, [vpl[part, pp] for pp in range(np_)])
+        for k in range(1, nl):
+            vec_copy(part, np_ - 1 + k).start()
+
+    def vec_sum(part):
+        for k in range(1, nl):
+            got(vln.at[part, line_from[k]], vs_r.at[part, np_ - 1 + k]).wait_recv()
+        return functools.reduce(lambda a, b: a + b, [vln[part, ll] for ll in range(nl)])
 
     def back_step(i):
         here = image_rows(i, G_BACK)
@@ -636,12 +666,15 @@
         g16 = gm.astype(BF16)
         gbr[here, :] = g16
         gatt[here, :] = dot_nn(g16, w_proj[...]).astype(BF16)
-        vec[2:3, 0:dim] += jnp.sum(dn * xhat, axis=0, keepdims=True)
-        vec[3:4, 0:dim] += jnp.sum(dn, axis=0, keepdims=True)
-        vec[4:5, 0:dim] += jnp.sum(g16.astype(F32), axis=0, keepdims=True)
-        vec[5:6, 0:dim] += jnp.sum(bfl, axis=0, keepdims=True)
+        vec[0, 0:1, 0:dim] += jnp.sum(dn * xhat, axis=0, keepdims=True)
+        vec[0, 1:2, 0:dim] += jnp.sum(dn, axis=0, keepdims=True)
+        vec[0, 2:3, 0:dim] += jnp.sum(g16.astype(F32), axis=0, keepdims=True)
+        vec[0, 3:4, 0:dim] += jnp.sum(bfl, axis=0, keepdims=True)
 
     over_images(back_step, G_BACK)
+    for j in range(chunks):
+        vec[0, 4 + j : 5 + j, :] = hid[0:1, j * chunk : (j + 1) * chunk]
+    vec_core(0)
 
     def attend_back(c):
         cols = lanes(c, 128)
@@ -664,8 +697,8 @@
             dq = (dot_tn(first, kp * head_scale[0]) + dot_tn(second, kp * head_scale[1])).astype(BF16)
             for b, grad in enumerate((dq, dk, dv)):
                 dqkv[here, lanes(3 * c + b, 128)] = grad
-            vec[6:7, cols] += jnp.sum(dq.astype(F32), axis=0, keepdims=True)
-            vec[7:8, cols] += jnp.sum(dv.astype(F32), axis=0, keepdims=True)
+            vec[1, 2:3, cols] += jnp.sum(dq.astype(F32), axis=0, keepdims=True)
+            vec[1, 3:4, cols] += jnp.sum(dv.astype(F32), axis=0, keepdims=True)
 
         start(0, even)
 
@@ -679,17 +712,20 @@
 
     def qkv_grad(c):
         grd[:, 0:384] = dot_tn(n1[...], dqkv[:, lanes(c, 384)])
-        grd[:, 384:512] = dot_tn(gbr[...], att[:, lanes(c, 128)])
+        grd[:, 384:512] = gproj[:, lanes(c, 128)]
         pack(("a", c))
         sib_copy(("a", c)).start()
 
+    send_line(("m", 0))
     send_plane(("m", 2))
+    gproj[...] = dot_tn(gbr[...], att[...])
 
     def pair_back(c, carry):
         attend_back(c)
 
         @pl.when(c == 0)
         def _():
+            vec_plane(0)
             send_line(("m", 1))
 
         @pl.when(c > 0)
@@ -697,6 +733,10 @@
             send_plane(("a", c - 1))
 
         @pl.when(c == 1)
+        def _():
+            vec_line(0)
+
+        @pl.when(c == 2)
         def _():
             send_line(("m", 2))
 
@@ -711,23 +751,20 @@
         dn = dot_nt(dqkv[here, :], w_qkv[...])
         xhat, rstd = norm_parts(xpad[here, :].astype(F32))
         gmid[here, :] = (gmid[here, :] + norm_back(dn, xhat, rstd, gain1)) * grad_scale
-        vec[0:1, 0:dim] += jnp.sum(dn * xhat, axis=0, keepdims=True)
-        vec[1:2, 0:dim] += jnp.sum(dn, axis=0, keepdims=True)
+        vec[1, 0:1, 0:dim] += jnp.sum(dn * xhat, axis=0, keepdims=True)
+        vec[1, 1:2, 0:dim] += jnp.sum(dn, axis=0, keepdims=True)
 
     first_part = images // G_LAST // 2
     lax.fori_loop(0, first_part, lambda i, carry: last_step(i) or carry, 0)
     send_plane(("a", 2))
     lax.fori_loop(first_part, images // G_LAST, lambda i, carry: last_step(i) or carry, 0)
-    send(vec, vsib, vs_s.at[0], vs_r.at[0], other_core)
+    vec_core(1)
 
     for i in range(images):
         stage[i * SEQ : (i + 1) * SEQ, :] = gmid[i * PAD : i * PAD + SEQ, :]
     gin_cp = pltpu.make_async_copy(stage.at[0:rows, :], gin_h, dma_sem.at[1])
     gin_cp.start()
-    got(vsib, vs_r.at[0]).wait_recv()
-    vpl[p] = vec[...] + vsib[...]
-    for k in range(1, np_):
-        send(vpl.at[p], vpl.at[p], vs_s.at[k], vs_r.at[k], plane_dev[k])
+    vec_plane(1)
     send_line(("a", 1))
 
     def out_step(i):
@@ -737,11 +774,7 @@
     half_out = images // G_OUT // 2
     lax.fori_loop(0, half_out, lambda i, carry: out_step(i) or carry, 0)
     send_line(("a", 2))
-    for k in range(1, np_):
-        got(vpl.at[plane_from[k]], vs_r.at[k]).wait_recv()
-    vln[l] = functools.reduce(lambda a, b: a + b, [vpl[pp] for pp in range(np_)])
-    for k in range(1, nl):
-        send(vln.at[l], vln.at[l], vs_s.at[np_ + k], vs_r.at[np_ + k], line_dev[k])
+    vec_line(1)
     lax.fori_loop(half_out, images // G_OUT, lambda i, carry: out_step(i) or carry, 0)
     for i in range(images):
         gmid[i * SEQ : (i + 1) * SEQ, :] = mid[i * PAD : i * PAD + SEQ, :]
@@ -757,13 +790,19 @@
     kept_o[...] = kept
     for pc in list(range(pairs, pairs + chunks)) + list(range(pairs)):
         sum_line(kind_of(pc))
-    for k in range(1, nl):
-        got(vln.at[line_from[k]], vs_r.at[np_ + k]).wait_recv()
-    vec_o[...] = functools.reduce(lambda a, b: a + b, [vln[ll] for ll in range(nl)])
+    early, last = vec_sum(0), vec_sum(1)
+    vec_o[0:2, :] = last[0:2, :]
+    vec_o[2:6, :] = early[0:4, :]
+    vec_o[6:8, :] = last[2:4, :]
+    vec_o[8:11, :] = early[4:7, :]
+    vec_o[11:16, :] = jnp.zeros((5, chunk), F32)
     out_cp.wait()
     gin_cp.wait()
     for pc in range(pairs + chunks):
         sums_sent(kind_of(pc))
+    for part in range(2):
+        for at in range(np_ + nl - 1):
+            vec_copy(part, at).wait_send()
     for cp in sends:
         cp.wait_send()
 
@@ -787,8 +826,11 @@
             loads.append(pltpu.make_async_copy(src.at[here, :], via.at[here, :], sems_in.at[j, k]))
             stores.append(pltpu.make_async_copy(via.at[here, :], dst.at[here, :], sems_out.at[j, k]))
     small = [pltpu.make_async_copy(src, dst, sems_a.at[k]) for k, (src, dst) in enumerate(zip(small_in, in_v))]
-    for cp in small + loads:
+    for cp in loads + small:
         cp.start()
+    for load, store in zip(loads, stores):
+        load.wait()
+        store.start()
     for cp in small:
         cp.wait()
     fin_a, fin_m, vec, kept = in_v[:4]
@@ -814,6 +856,10 @@
 
     pairs = fin_a.shape[0]
 
+    def begin(a, b):
+        for cp in results[a:b]:
+            cp.start()
+
     def over_pairs(block, lane_at):
         return jnp.concatenate(
             [fin_a[c, block * r : (block + 1) * r, lane_at : lane_at + 64] for c in range(pairs)], axis=1
@@ -822,10 +868,15 @@
     update(over_pairs(0, 0), qkv, q_o, 0.08, matrix_decay, 0)
     update(over_pairs(0, 64), qkv, q_o, 0.08, matrix_decay, 1)
     update(over_pairs(1, 0), qkv, q_o, 0.08, matrix_decay, 2)
+    begin(0, 3)
     update(over_pairs(1, 64), proj, p_o, 0.8, matrix_decay)
+    begin(3, 6)
     update(jnp.concatenate([fin_m[j, 0:r, :] for j in range(chunks)], axis=1), fc1, a_o, 0.08, matrix_decay)
+    begin(6, 9)
     update(jnp.concatenate([fin_m[j, r : 2 * r, :] for j in range(chunks)], axis=1), fc2, c_o, 0.04, matrix_decay)
+    begin(9, 12)
     update(vec[0:6, 0 : norm[0].shape[1]], norm, n_o, 0.5, 0.0)
+    begin(12, 15)
 
     def pick(row, col, cols):
         return jnp.where(
@@ -835,11 +886,7 @@
     bias_parts = [pick(row, 128 * c, 64) for row in (6, 7) for c in range(pairs)]
     bias_parts += [pick(8 + j, 0, width) for j in range(chunks)]
     update(jnp.concatenate(bias_parts, axis=1), bias, b_o, 0.5, 0.0)
-    for cp in results:
-        cp.start()
-    for load, store in zip(loads, stores):
-        load.wait()
-        store.start()
+    begin(15, 18)
     for cp in results + stores:
         cp.wait()
 
@@ -894,6 +941,7 @@
         pltpu.VMEM((dim, chunks * chunk), BF16),
         pltpu.VMEM((dim, chunks * chunk), BF16),
         pltpu.VMEM((dim, 2 * chunk), F32),
+        pltpu.VMEM((dim, dim), F32),
         pltpu.VMEM((pairs, np_ * nl, slot_a, 128), BF16),
         pltpu.VMEM((chunks, np_ * nl, slot_m, width), BF16),
         pltpu.VMEM((pairs, np_ * nl, slot_a, 128), BF16),
@@ -909,10 +957,10 @@
         pltpu.VMEM((np_, 8, 128), F32),
         pltpu.VMEM((8, chunks * chunk), F32),
         pltpu.VMEM((8, chunks * chunk), F32),
-        pltpu.VMEM((16, chunk), F32),
-        pltpu.VMEM((16, chunk), F32),
-        pltpu.VMEM((np_, 16, chunk), F32),
-        pltpu.VMEM((nl, 16, chunk), F32),
+        pltpu.VMEM((2, 8, chunk), F32),
+        pltpu.VMEM((2, 8, chunk), F32),
+        pltpu.VMEM((2, np_, 8, chunk), F32),
+        pltpu.VMEM((2, nl, 8, chunk), F32),
         pltpu.VMEM((-(-(rows - SEQ + PAD) // 16) * 16, dim), F32),
         pltpu.VMEM((padded, dim), F32),
         pltpu.VMEM((padded, dim), F32),
@@ -948,8 +996,8 @@
         dma((nl,)),
         dma((np_,)),
         dma((np_,)),
-        dma((np_ + nl,)),
-        dma((np_ + nl,)),
+        dma((2, np_ + nl - 1)),
+        dma((2, np_ + nl - 1)),
     ]
     out, gin, fin_a, fin_m, vec, kept = pl.pallas_call(
         functools.partial(kernel, nl, np_),

time: 81 us -> 77.5 us (0.957)
  Pallas kernels: 80 us -> 76.5 us
    pallas_call x1, Pallas kernels: 74.6 us -> 71.6 us  [body(): pl.pallas_call(functools.partial(kernel, nl, np_), out_shape=large + sums...]
where the time goes in v1:
time: 77.5 us; the launch traced here: 77.4 us
  Pallas kernels  76.5 us (99%)
  between operations  0.83 us (1%)
    pallas_call x1, Pallas kernels, body(): pl.pallas_call(functools.partial(kernel, nl, np_), out_shape=large + sums...  71.6 us
    pallas_call x1, Pallas kernels, body(): pl.pallas_call(functools.partial(update_kernel, rows * 2.0 * n), out_shap...  4.99 us

profile of v1, /device:TPU:0, one launch (start us, length us, event | category | flops | bytes accessed | tf_op | source)
XLA Modules:
  0.0 77.4 jit_solution(5153815045333233926)
XLA Ops:
  0.7 71.6 %shard_map.388 = (bf16[1584,384]{1,0:T(8,128)(2,1)}, f32[1584,384]{1,0:T(8,128)}, f32[3,48,128]{2,1,0:T(8,128)}, f32[3,48,256]{2,1,0:T(8,128)}, f32[16,512]{1,0:T(8,128)}, /*index=5*/f32[8,128]{1,0:T(8,128)}) custom-call(bf16[1584,384]{1,0:T(8,128)(2,1)} %x_h.1, s32[3168]{0:T(1024)} %keep_h.1, bf16[1584,384]{1,0:T(8,128)(2,1)} %cot_h.1, ...), custom_call_target="tpu_custom_call" | custom-call | tf_op jit(solution)/shard_map/pallas_call | solution.py:1002
  72.2 5.0 %shard_map.389 = (bf16[1584,384]{1,0:T(8,128)(2,1)}, f32[1584,384]{1,0:T(8,128)}, f32[3,24,192]{2,1,0:T(8,128)}, f32[3,24,192]{2,1,0:T(8,128)}, f32[3,24,192]{2,...) custom-call(f32[3,48,128]{2,1,0:T(8,128)} %get-tuple-element.54.refs, ...), custom_call_target="tpu_custom_call" | custom-call | tf_op jit(solution)/shard_map/pallas_call | solution.py:1026

commit v2 on v1

--- a/solution.py
+++ b/solution.py
@@ -127,7 +127,6 @@
     biases,
     hid,
     vec,
-    vsib,
     vpl,
     vln,
     stage,
@@ -190,6 +189,7 @@
     line_dev = [{"dp": ll * np_ + p} for ll in line_peer]
     plane_dev = [{"dp": l * np_ + pp} for pp in plane_peer]
     other_core = {"tp": o}
+    cross_dev = [{"dp": l * np_ + pp, "tp": o} for pp in plane_peer]
     block = nl * np_
 
     def slot_at(tt, pp, ll):
@@ -215,6 +215,7 @@
         pl.semaphore_signal(barrier, inc=1, device_id=line_dev[k], device_id_type=MESH)
     for k in range(1, np_):
         pl.semaphore_signal(barrier, inc=1, device_id=plane_dev[k], device_id_type=MESH)
+        pl.semaphore_signal(barrier, inc=1, device_id=cross_dev[k], device_id_type=MESH)
     pl.semaphore_signal(barrier, inc=1, device_id=other_core, device_id_type=MESH)
 
     def kind_of(pc):
@@ -267,7 +268,7 @@
     count = jnp.sum(jnp.sum(mkt[...], axis=1, keepdims=True), axis=0, keepdims=True)
     cntl[l] = jnp.broadcast_to(count, cntl.shape[1:])
 
-    pl.semaphore_wait(barrier, nl - 1 + np_ - 1 + 1)
+    pl.semaphore_wait(barrier, nl - 1 + 2 * (np_ - 1) + 1)
 
     def remote(src, dst, ssem, rsem, device):
         return pltpu.make_async_remote_copy(
@@ -296,32 +297,43 @@
         pc, here = sem_of(piece), w_buf(piece).at[pl.ds(slot_at(t, plane_from[k], 0), nl)]
         return remote(here, here, ag_s.at[pc], ag_cr.at[pc], other_core)
 
-    def own_to_plane(piece):
-        for k in range(1, np_):
-            plane_copy(piece, 0, k).start()
+    def row_copy(piece, k):
+        pc, here = sem_of(piece), w_buf(piece).at[pl.ds(slot_at(t, p, 0), nl)]
+        return remote(here, here, ag_s.at[pc], ag_pr.at[pc, k - 1], plane_dev[k])
+
+    def half_copy(piece):
+        pc, here = sem_of(piece), w_buf(piece).at[pl.ds(t * block, block)]
+        return remote(here, here, ag_s.at[pc], ag_cr.at[pc], other_core)
 
     def start_piece(pc):
         piece = kind_of(pc)
         for k in range(1, nl):
             line_copy(piece, k).start()
-        if piece[0] == "a":
-            own_to_plane(piece)
+        if pc == 0:
+            for k in range(1, np_):
+                plane_copy(piece, 0, k).start()
 
     def line_done(pc):
         piece = kind_of(pc)
-        if piece[0] == "m":
-            own_to_plane(piece)
         for k in range(1, nl):
             got(w_buf(piece).at[slot_at(t, p, line_from[k])], ag_lr.at[pc, k - 1]).wait_recv()
-            for kp in range(1, np_):
-                plane_copy(piece, k, kp).start()
-        core_copy(piece, 0).start()
+            if pc == 0:
+                for kp in range(1, np_):
+                    plane_copy(piece, k, kp).start()
+        if pc == 0:
+            core_copy(piece, 0).start()
+        else:
+            for k in range(1, np_):
+                row_copy(piece, k).start()
 
     def plane_done(pc):
         piece = kind_of(pc)
         for k in range(1, np_):
             got(w_buf(piece).at[pl.ds(slot_at(t, plane_from[k], 0), nl)], ag_pr.at[pc, k - 1]).wait_recv()
-            core_copy(piece, k).start()
+            if pc == 0:
+                core_copy(piece, k).start()
+        if pc > 0:
+            half_copy(piece).start()
 
     def core_done(piece):
         got(w_buf(piece).at[pl.ds(o * block, block)], ag_cr.at[sem_of(piece)]).wait_recv()
@@ -626,33 +638,43 @@
 
     lax.fori_loop(0, chunks, chunk_step, 0)
 
+    own_vec = t * np_ + p
+    near = 2 * np_ - 1
+
     def vec_copy(part, at):
         ssem, rsem = vs_s.at[part, at], vs_r.at[part, at]
+        here = (vpl if at < near else vln).at[part, own_vec if at < near else l]
         if at == 0:
-            return remote(vec.at[part], vsib.at[part], ssem, rsem, other_core)
-        if at < np_:
-            return remote(vpl.at[part, p], vpl.at[part, p], ssem, rsem, plane_dev[at])
-        return remote(vln.at[part, l], vln.at[part, l], ssem, rsem, line_dev[at - np_ + 1])
-
-    def vec_core(part):
-        vec_copy(part, 0).start()
-
-    def vec_plane(part):
-        got(vsib.at[part], vs_r.at[part, 0]).wait_recv()
-        vpl[part, p] = vec[part] + vsib[part]
-        for k in range(1, np_):
-            vec_copy(part, k).start()
+            device = other_core
+        elif at < np_:
+            device = plane_dev[at]
+        elif at < near:
+            device = cross_dev[at - np_ + 1]
+        else:
+            device = line_dev[at - near + 1]
+        return remote(here, here, ssem, rsem, device)
+
+    def vec_start(part):
+        vpl[part, own_vec] = vec[part]
+        for at in range(near):
+            vec_copy(part, at).start()
 
     def vec_line(part):
-        for k in range(1, np_):
-            got(vpl.at[part, plane_from[k]], vs_r.at[part, k]).wait_recv()
-        vln[part, l] = functools.reduce(lambda a, b: a + b, [vpl[part, pp] for pp in range(np_)])
+        for at in range(near):
+            if at == 0:
+                slot = o * np_ + p
+            elif at < np_:
+                slot = t * np_ + plane_from[at]
+            else:
+                slot = o * np_ + plane_from[at - np_ + 1]
+            got(vpl.at[part, slot], vs_r.at[part, at]).wait_recv()
+        vln[part, l] = functools.reduce(lambda a, b: a + b, [vpl[part, at] for at in range(2 * np_)])
         for k in range(1, nl):
-            vec_copy(part, np_ - 1 + k).start()
+            vec_copy(part, near - 1 + k).start()
 
     def vec_sum(part):
         for k in range(1, nl):
-            got(vln.at[part, line_from[k]], vs_r.at[part, np_ - 1 + k]).wait_recv()
+            got(vln.at[part, line_from[k]], vs_r.at[part, near - 1 + k]).wait_recv()
         return functools.reduce(lambda a, b: a + b, [vln[part, ll] for ll in range(nl)])
 
     def back_step(i):
@@ -674,7 +696,7 @@
     over_images(back_step, G_BACK)
     for j in range(chunks):
         vec[0, 4 + j : 5 + j, :] = hid[0:1, j * chunk : (j + 1) * chunk]
-    vec_core(0)
+    vec_start(0)
 
     def attend_back(c):
         cols = lanes(c, 128)
@@ -725,7 +747,6 @@
 
         @pl.when(c == 0)
         def _():
-            vec_plane(0)
             send_line(("m", 1))
 
         @pl.when(c > 0)
@@ -758,13 +779,12 @@
     lax.fori_loop(0, first_part, lambda i, carry: last_step(i) or carry, 0)
     send_plane(("a", 2))
     lax.fori_loop(first_part, images // G_LAST, lambda i, carry: last_step(i) or carry, 0)
-    vec_core(1)
+    vec_start(1)
 
     for i in range(images):
         stage[i * SEQ : (i + 1) * SEQ, :] = gmid[i * PAD : i * PAD + SEQ, :]
     gin_cp = pltpu.make_async_copy(stage.at[0:rows, :], gin_h, dma_sem.at[1])
     gin_cp.start()
-    vec_plane(1)
     send_line(("a", 1))
 
     def out_step(i):
@@ -775,20 +795,31 @@
     lax.fori_loop(0, half_out, lambda i, carry: out_step(i) or carry, 0)
     send_line(("a", 2))
     vec_line(1)
+    early_rows = images // 2 * SEQ // 16 * 16
+
+    def take_out(first, last, row, stop, sem):
+        for i in range(first, last):
+            gmid[i * SEQ : (i + 1) * SEQ, :] = mid[i * PAD : i * PAD + SEQ, :]
+
+        def cast_out(c, carry):
+            at_row = pl.ds(pl.multiple_of(row + c * 16, 16), 16)
+            n2[at_row, :] = gmid[at_row, :].astype(BF16)
+            return carry
+
+        lax.fori_loop(0, (stop - row) // 16, cast_out, 0, unroll=True)
+        here = pl.ds(row, stop - row)
+        cp = pltpu.make_async_copy(n2.at[here, :], out_h.at[here, :], dma_sem.at[sem])
+        cp.start()
+        return cp
+
+    out_first = take_out(0, images // 2, 0, early_rows, 0)
+    for pc in range(pairs, pairs + chunks):
+        sum_line(kind_of(pc))
+    sum_line(kind_of(0))
     lax.fori_loop(half_out, images // G_OUT, lambda i, carry: out_step(i) or carry, 0)
-    for i in range(images):
-        gmid[i * SEQ : (i + 1) * SEQ, :] = mid[i * PAD : i * PAD + SEQ, :]
-
-    def cast_out(c, carry):
-        at_row = pl.ds(pl.multiple_of(c * 16, 16), 16)
-        n2[at_row, :] = gmid[at_row, :].astype(BF16)
-        return carry
-
-    lax.fori_loop(0, rows // 16, cast_out, 0)
-    out_cp = pltpu.make_async_copy(n2.at[0:rows, :], out_h, dma_sem.at[0])
-    out_cp.start()
+    out_rest = take_out(images // 2, images, early_rows, rows, 3)
     kept_o[...] = kept
-    for pc in list(range(pairs, pairs + chunks)) + list(range(pairs)):
+    for pc in range(1, pairs):
         sum_line(kind_of(pc))
     early, last = vec_sum(0), vec_sum(1)
     vec_o[0:2, :] = last[0:2, :]
@@ -796,12 +827,13 @@
     vec_o[6:8, :] = last[2:4, :]
     vec_o[8:11, :] = early[4:7, :]
     vec_o[11:16, :] = jnp.zeros((5, chunk), F32)
-    out_cp.wait()
+    out_first.wait()
+    out_rest.wait()
     gin_cp.wait()
     for pc in range(pairs + chunks):
         sums_sent(kind_of(pc))
     for part in range(2):
-        for at in range(np_ + nl - 1):
+        for at in range(near + nl - 1):
             vec_copy(part, at).wait_send()
     for cp in sends:
         cp.wait_send()
@@ -958,8 +990,7 @@
         pltpu.VMEM((8, chunks * chunk), F32),
         pltpu.VMEM((8, chunks * chunk), F32),
         pltpu.VMEM((2, 8, chunk), F32),
-        pltpu.VMEM((2, 8, chunk), F32),
-        pltpu.VMEM((2, np_, 8, chunk), F32),
+        pltpu.VMEM((2, 2 * np_, 8, chunk), F32),
         pltpu.VMEM((2, nl, 8, chunk), F32),
         pltpu.VMEM((-(-(rows - SEQ + PAD) // 16) * 16, dim), F32),
         pltpu.VMEM((padded, dim), F32),
@@ -980,7 +1011,7 @@
         pltpu.VMEM((padded, chunks * chunk), BF16),
         pltpu.VMEM((padded, chunks * chunk), BF16),
         pltpu.VMEM((padded, 3 * dim), BF16),
-        dma((3,)),
+        dma((4,)),
         dma((7,)),
         dma((pieces,)),
         dma((pieces, nl - 1)),
@@ -996,8 +1027,8 @@
         dma((nl,)),
         dma((np_,)),
         dma((np_,)),
-        dma((2, np_ + nl - 1)),
-        dma((2, np_ + nl - 1)),
+        dma((2, 2 * np_ + nl - 2)),
+        dma((2, 2 * np_ + nl - 2)),
     ]
     out, gin, fin_a, fin_m, vec, kept = pl.pallas_call(
         functools.partial(kernel, nl, np_),

time: 77.5 us -> 76.9 us (level)
  no operation moved by 1% of the time
where the time goes in v2:
time: 76.9 us; the launch traced here: 76.8 us
  Pallas kernels  75.9 us (99%)
  between operations  0.83 us (1%)
    pallas_call x1, Pallas kernels, body(): pl.pallas_call(functools.partial(kernel, nl, np_), out_shape=large + sums...  70.9 us
    pallas_call x1, Pallas kernels, body(): pl.pallas_call(functools.partial(update_kernel, rows * 2.0 * n), out_shap...  4.99 us

profile of v2, /device:TPU:0, one launch (start us, length us, event | category | flops | bytes accessed | tf_op | source)
XLA Modules:
  0.0 76.8 jit_solution(15048705630402243925)
XLA Ops:
  0.7 70.9 %shard_map.388 = (bf16[1584,384]{1,0:T(8,128)(2,1)}, f32[1584,384]{1,0:T(8,128)}, f32[3,48,128]{2,1,0:T(8,128)}, f32[3,48,256]{2,1,0:T(8,128)}, f32[16,512]{1,0:T(8,128)}, /*index=5*/f32[8,128]{1,0:T(8,128)}) custom-call(bf16[1584,384]{1,0:T(8,128)(2,1)} %x_h.1, s32[3168]{0:T(1024)} %keep_h.1, bf16[1584,384]{1,0:T(8,128)(2,1)} %cot_h.1, ...), custom_call_target="tpu_custom_call" | custom-call | tf_op jit(solution)/shard_map/pallas_call | solution.py:1033
  71.6 5.0 %shard_map.389 = (bf16[1584,384]{1,0:T(8,128)(2,1)}, f32[1584,384]{1,0:T(8,128)}, f32[3,24,192]{2,1,0:T(8,128)}, f32[3,24,192]{2,1,0:T(8,128)}, f32[3,24,192]{2,...) custom-call(f32[3,48,128]{2,1,0:T(8,128)} %get-tuple-element.54.refs, ...), custom_call_target="tpu_custom_call" | custom-call | tf_op jit(solution)/shard_map/pallas_call | solution.py:1057
